TPU v7x, 32 devices: a whole 2x2x4 slice. The times are simulated.
32 devices in a mesh: loop: 4 (over y, x), grp: 8 (over z, core).
Axes of the slice: x: 2, y: 2, z: 4, core: 2. Of those that a mesh axis runs over, the one named last changes fastest.
Arguments:
- queries: bfloat16 [512, 1024], P(('loop', 'grp')), may hold values from -100 to 100
- landmarks: bfloat16 [2048, 1024], P(('loop', 'grp')), may hold values from -20 to 20
- labels: bfloat16 [2048, 128], P(('loop', 'grp')), may hold values from -6 to 6
- tile_mask: int32 [4, 32], replicated, may hold values from 0 to 1, as said below
Outputs:
- label_scores: bfloat16 [512, 128], P(('loop', 'grp'))
Inputs may be any that keep to these rules, and one draw needn't show every extreme that they name: `tile_mask`: every query tile lists at least one landmark tile.
All inputs are finite; a program needn't handle non-finite values.
Results may differ from a plain program's by a relative error of at most 0.0065.
Values may be sent and summed in bfloat16 or wider, within the bound.
A program may use at most 64 MiB of HBM per device.

v0:
```python
import math

import jax
import jax.numpy as jnp
from jax import lax
from jax.sharding import PartitionSpec as P


def from_behind(value, axis, steps):
    count = lax.axis_size(axis)
    pairs = [(source, (source + steps) % count) for source in range(count)]
    return lax.ppermute(value, axis, pairs)


def combined_all(part, axis, combine):
    gathered = jax.tree.map(lambda a: lax.all_gather(a, axis), part)

    def take(source):
        return jax.tree.map(lambda a: lax.dynamic_index_in_dim(a, source, 0, False), gathered)

    return lax.fori_loop(
        1, lax.axis_size(axis), lambda source, state: combine(state, take(source)), take(0)
    )


def combine(first, second):
    first_max, first_sum, first_labels = first
    second_max, second_sum, second_labels = second
    joint_max = jnp.maximum(first_max, second_max)
    first_keep = jnp.exp(first_max - joint_max)
    second_keep = jnp.exp(second_max - joint_max)
    return (
        joint_max,
        first_sum * first_keep + second_sum * second_keep,
        first_labels * first_keep[:, None] + second_labels * second_keep[:, None],
    )


def local(queries, landmarks, labels, tile_mask):
    query_slab = lax.all_gather(queries, "grp", axis=0, tiled=True)
    n_loop = lax.axis_size("loop")
    n_grp = lax.axis_size("grp")
    cycle_pos = lax.axis_index("loop")
    column = lax.axis_index("grp")
    feature_width = landmarks.shape[1]
    slab_rows = query_slab.shape[0]
    classes = labels.shape[1]
    scale_factor = 4.0 / math.sqrt(feature_width)
    listed_row = lax.dynamic_index_in_dim(tile_mask, cycle_pos, 0, keepdims=False)
    packed = jnp.concatenate([landmarks, labels], axis=1)

    def absorb(carried, packed_tile, source):
        listed = (
            lax.dynamic_index_in_dim(listed_row, source * n_grp + column, 0, keepdims=False) > 0
        )
        row_max, weight_sum, label_sum = carried
        land_rows = packed_tile[:, :feature_width]
        label_rows = packed_tile[:, feature_width:]
        land_f = land_rows.astype(jnp.float32)
        half_norm = 0.5 * jnp.sum(land_f * land_f, axis=1)
        logits = lax.dot_general(
            query_slab, land_rows, (((1,), (1,)), ((), ())), preferred_element_type=jnp.float32
        )
        logits = (logits - half_norm[None, :]) * scale_factor
        new_max = jnp.where(listed, jnp.maximum(row_max, jnp.max(logits, axis=1)), row_max)
        kernel = jnp.where(listed, jnp.exp(logits - new_max[:, None]), jnp.float32(0.0))
        rescale = jnp.exp(row_max - new_max)
        new_labels = label_sum * rescale[:, None] + jnp.dot(
            kernel.astype(jnp.bfloat16), label_rows, preferred_element_type=jnp.float32
        )
        return (new_max, weight_sum * rescale + jnp.sum(kernel, axis=1), new_labels)

    initial = (
        jnp.full((slab_rows,), -1e30, jnp.float32),
        jnp.zeros((slab_rows,), jnp.float32),
        jnp.zeros((slab_rows, classes), jnp.float32),
    )
    carried = absorb(initial, packed, cycle_pos)
    half_steps = (n_loop - 1) // 2

    def both_step(offset, state):
        current, ahead, behind = state
        ahead = from_behind(ahead, "loop", 1)
        behind = from_behind(behind, "loop", -1)
        current = absorb(current, ahead, (cycle_pos - offset) % n_loop)
        current = absorb(current, behind, (cycle_pos + offset) % n_loop)
        return (current, ahead, behind)

    carried, ahead, behind = lax.fori_loop(1, half_steps + 1, both_step, (carried, packed, packed))
    ahead = from_behind(ahead, "loop", 1)
    carried = absorb(carried, ahead, (cycle_pos - half_steps - 1) % n_loop)
    row_max, weight_sum, label_sum = combined_all(carried, "grp", combine)
    result = (label_sum / weight_sum[:, None]).astype(jnp.bfloat16)
    return lax.dynamic_slice_in_dim(result, column * queries.shape[0], queries.shape[0], 0)


def solution(mesh):
    in_specs = (P(("loop", "grp"), None), P(("loop", "grp"), None), P(("loop", "grp"), None), P())
    out_specs = P(("loop", "grp"), None)
    return jax.shard_map(local, mesh=mesh, in_specs=in_specs, out_specs=out_specs, check_vma=False)
```

profile of v0, /device:TPU:0, one launch (start us, length us, event | category | flops | bytes accessed | tf_op | source)
XLA Modules:
  0.0 70.1 jit_solution(17377897367747982764)
XLA Ops:
  0.0 0.9 %constant_dynamic-update-slice_fusion.1 = bf16[64,1152]{1,0:T(8,128)(2,1)S(1)} fusion(bf16[64,1024]{1,0:T(8,128)(2,1)} %param.7), kind=kLoop, calls=%fused_computation.64 | loop fusion | bytes 262144
  1.0 3.0 %collective-permute-start = (bf16[64,1152]{1,0:T(8,128)(2,1)S(1)}, bf16[64,1152]{1,0:T(8,128)(2,1)S(1)}, u32[]{:S(2)}, u32[]{:S(2)}) collective-permute-start(bf16[64,1152]{1,0:T(8,128)(2,1)S(1)} %constant_dynamic-update-slice_fusion), channel_id=1, source_target_pairs={{0,8},{8,16},{16,24},{24,0},{1,9},{9,17},{17,25},{25,1},{2,10},{10... | collective-permute-start | bytes 442376 | tf_op jit(solution)/shard_map/while/body/eval_jaxpr/ppermute | solution.py:12
  4.0 1.0 %collective-permute-start.1 = (bf16[64,1152]{1,0:T(8,128)(2,1)S(1)}, bf16[64,1152]{1,0:T(8,128)(2,1)S(1)}, u32[]{:S(2)}, u32[]{:S(2)}) collective-permute-start(bf16[64,1152]{1,0:T(8,128)(2,1)S(1)} %constant_dynamic-update-slice_fusion), channel_id=1, source_target_pairs={{0,24},{8,0},{16,8},{24,16},{1,25},{9,1},{17,9},{25,17},{2,26},{10... | collective-permute-start | bytes 442376 | tf_op jit(solution)/shard_map/while/body/eval_jaxpr/ppermute | solution.py:12
  5.0 0.1 multiply_reduce_fusion.3
  5.2 0.5 copy-done.3
  5.7 0.7 fusion.59
  8.2 14.9 %all_gather.17 = bf16[128,1024]{1,0:T(8,128)(2,1)S(1)} all-gather(bf16[16,1024]{1,0:T(8,128)(2,1)S(1)} %copy-done.1), channel_id=1, replica_groups=mesh['loop'=4,'grp'=8] {'grp'}, dimensions={0}, use_global_device_ids=true | all-gather | bytes 294912 | tf_op jit(solution)/shard_map/all_gather | solution.py:40
  23.6 0.2 fusion.62
  23.9 0.1 multiply_reduce_fusion.2
  24.0 0.1 multiply_reduce_fusion.1
  24.2 0.2 fusion.61
  24.4 0.2 fusion.60
  24.7 0.2 fusion.9
  24.9 0.6 collective-permute-start.2
  25.5 0.2 fusion.26
  25.8 6.1 %collective-permute-done.2 = bf16[64,1152]{1,0:T(8,128)(2,1)S(1)} collective-permute-done((bf16[64,1152]{1,0:T(8,128)(2,1)S(1)}, bf16[64,1152]{1,0:T(8,128)(2,1)S(1)}, u32[]{:S(2)}, u32[]{:S(2)}) %collective-permute-start.2) | collective-permute-done | bytes 147488 | tf_op jit(solution)/shard_map/ppermute | solution.py:12
  31.9 0.1 multiply_reduce_fusion
  32.1 0.2 fusion.63
  32.3 0.2 fusion.8
  32.5 0.2 convolution_add_fusion
  32.7 14.9 %all-gather = f32[1024,128]{1,0:T(8,128)S(1)} all-gather(f32[128,128]{1,0:T(8,128)S(1)} %convolution_add_fusion), channel_id=2, replica_groups=mesh['loop'=4,'grp'=8] {'grp'}, dimensions={0}, use_global_device_ids=true | all-gather | bytes 589824 | tf_op jit(solution)/shard_map/all_gather | solution.py:16
  47.6 11.9 %all-gather.2 = f32[8,1,128]{2,1,0:T(1,128)S(1)} all-gather(f32[1,1,128]{2,1,0:T(1,128)S(1)} %get-tuple-element.241), channel_id=1, replica_groups=mesh['loop'=4,'grp'=8] {'grp'}, dimensions={0}, use_global_device_ids=true | all-gather | bytes 4608 | tf_op jit(solution)/shard_map/all_gather | solution.py:16
  59.5 8.6 %all-gather.1 = f32[8,1,128]{2,1,0:T(1,128)S(1)} all-gather(f32[1,1,128]{2,1,0:T(1,128)S(1)} %get-tuple-element.242), channel_id=1, replica_groups=mesh['loop'=4,'grp'=8] {'grp'}, dimensions={0}, use_global_device_ids=true | all-gather | bytes 4608 | tf_op jit(solution)/shard_map/all_gather | solution.py:16
  68.1 1.1 %while.12 = (s32[]{:T(128)}, f32[128]{0:T(128)S(1)}, f32[128]{0:T(128)S(1)}, f32[128,128]{1,0:T(8,128)S(1)}, f32[8,128]{1,0:T(8,128)S(1)}, /*index=5*/f32[8,128]...) while((s32[]{:T(128)}, f32[128]{0:T(128)S(1)}, f32[128]{0:T(128)S(1)}, ...), condition=%wide.region_13.14_spmd, body=%wide.region_12.13_spmd.sunk | while | flops 49925 | bytes 201879 | solution.py:21
  68.2 0.1 fusion.73
  68.3 0.1 fusion.73
  68.5 0.1 fusion.73
  68.7 0.1 fusion.73
  68.8 0.1 fusion.73
  69.0 0.1 fusion.73
  69.2 0.1 fusion.73
  69.4 0.7 fusion.45
  (33 shorter events, 0.5 us)
Async XLA Ops:
  0.0 0.9 %copy-start.2 = (bf16[64,128]{1,0:T(8,128)(2,1)S(1)}, bf16[64,128]{1,0:T(8,128)(2,1)}, u32[]{:S(2)}) copy-start(bf16[64,128]{1,0:T(8,128)(2,1)} %param.8) | copy-start | bytes 49156
  0.9 4.0 %copy-start = (bf16[64,1024]{1,0:T(8,128)(2,1)S(1)}, bf16[64,1024]{1,0:T(8,128)(2,1)}, u32[]{:S(2)}) copy-start(bf16[64,1024]{1,0:T(8,128)(2,1)} %param.7) | copy-start | bytes 393220
  1.0 22.9 %collective-permute-start = (bf16[64,1152]{1,0:T(8,128)(2,1)S(1)}, bf16[64,1152]{1,0:T(8,128)(2,1)S(1)}, u32[]{:S(2)}, u32[]{:S(2)}) collective-permute-start(bf16[64,1152]{1,0:T(8,128)(2,1)S(1)} %constant_dynamic-update-slice_fusion), channel_id=1, source_target_pairs={{0,8},{8,16},{16,24},{24,0},{1,9},{9,17},{17,25},{25,1},{2,10},{10... | collective-permute-start | bytes 442376 | tf_op jit(solution)/shard_map/while/body/eval_jaxpr/ppermute | solution.py:12
  4.0 20.1 %collective-permute-start.1 = (bf16[64,1152]{1,0:T(8,128)(2,1)S(1)}, bf16[64,1152]{1,0:T(8,128)(2,1)S(1)}, u32[]{:S(2)}, u32[]{:S(2)}) collective-permute-start(bf16[64,1152]{1,0:T(8,128)(2,1)S(1)} %constant_dynamic-update-slice_fusion), channel_id=1, source_target_pairs={{0,24},{8,0},{16,8},{24,16},{1,25},{9,1},{17,9},{25,17},{2,26},{10... | collective-permute-start | bytes 442376 | tf_op jit(solution)/shard_map/while/body/eval_jaxpr/ppermute | solution.py:12
  5.0 0.7 copy-start.3
  5.1 3.1 %copy-start.1 = (bf16[16,1024]{1,0:T(8,128)(2,1)S(1)}, bf16[16,1024]{1,0:T(8,128)(2,1)}, u32[]{:S(2)}) copy-start(bf16[16,1024]{1,0:T(8,128)(2,1)} %param.6) | copy-start | bytes 98308
  24.9 7.1 %collective-permute-start.2 = (bf16[64,1152]{1,0:T(8,128)(2,1)S(1)}, bf16[64,1152]{1,0:T(8,128)(2,1)S(1)}, u32[]{:S(2)}, u32[]{:S(2)}) collective-permute-start(bf16[64,1152]{1,0:T(8,128)(2,1)S(1)} %collective-permute-done), channel_id=1, source_target_pairs={{0,8},{8,16},{16,24},{24,0},{1,9},{9,17},{17,25},{25,1},{2,10},{10... | collective-permute-start | bytes 442376 | tf_op jit(solution)/shard_map/ppermute | solution.py:12
where the time goes:
time: 70.3 us; the launch traced here: 70.1 us
  blocking collectives  50.2 us (71%)
  waiting for transfers between devices  6.15 us (9%)
  starting transfers between devices  4.66 us (7%)
  between operations  2.6 us (4%)
  other arithmetic  2.35 us (3%)
  local copies, waits for them, and re-layouts  2.22 us (3%)
  matrix products  1.68 us (2%)
    all_gather x3, blocking collectives, combined_all(): gathered = jax.tree.map(lambda a: lax.all_gather(a, axis), part)  35.4 us
    all_gather x1, blocking collectives, local(): query_slab = lax.all_gather(queries, 'grp', axis=0, tiled=True)  14.9 us
    ppermute x3, waiting for transfers between devices, from_behind(): return lax.ppermute(value, axis, pairs)  6.15 us
    ppermute x3, starting transfers between devices, from_behind(): return lax.ppermute(value, axis, pairs)  4.66 us
    unnamed x9, local copies, waits for them, and re-layouts  1.46 us
  transfers between devices with their start and end apart: 3, of which 1 were waited for; matrix products, arithmetic and copies ran while one was open for 2% of the time, Pallas kernels for 0%

commit v1 on v0

v1 whole, which is shorter than its diff:
```python
import functools
import math

import jax
import jax.numpy as jnp
from jax import lax
from jax.experimental import pallas as pl
from jax.experimental.pallas import tpu as pltpu
from jax.sharding import PartitionSpec as P

MESH = pl.DeviceIdType.MESH
CHUNKS = 2


def three_terms(value):
    first = value.astype(jnp.bfloat16)
    rest = value - first.astype(jnp.float32)
    second = rest.astype(jnp.bfloat16)
    third = (rest - second.astype(jnp.float32)).astype(jnp.bfloat16)
    return [t.astype(jnp.float32) for t in (first, second, third)]


def kernel(
    dims,
    mask_ref,
    q_hbm,
    land_hbm,
    lab_hbm,
    out_ref,
    q_all,
    land_all,
    lab_all,
    part,
    got,
    own_sem,
    qz_send,
    qz_recv,
    qy_send,
    qy_recv,
    lx_send,
    lx_recv,
    bx_send,
    bx_recv,
    ls_send,
    ls_recv,
    bs_send,
    bs_recv,
    p_send,
    p_recv,
):
    n_hi, n_lo, n_z, n_core = dims
    n_grp = n_z * n_core
    rows, width = q_hbm.shape
    land_rows = land_hbm.shape[0]
    classes = lab_hbm.shape[1]
    tiles = n_lo * n_core
    loop = lax.axis_index("loop")
    grp = lax.axis_index("grp")
    hi, lo = loop // n_lo, lax.rem(loop, n_lo)
    z, core = grp // n_core, lax.rem(grp, n_core)

    def device(hi_, lo_, z_, core_):
        return (hi_ * n_lo + lo_, z_ * n_core + core_)

    def plus(a, d, n):
        return lax.rem(a + d + n, n)

    def remote(src, dst, send, recv, dev):
        return pltpu.make_async_remote_copy(
            src_ref=src, dst_ref=dst, send_sem=send, recv_sem=recv, device_id=dev, device_id_type=MESH
        )

    mine_q = hi * n_z + z
    mine_l = lo * n_core + core
    local = [
        pltpu.make_async_copy(q_hbm, q_all.at[mine_q], own_sem.at[0]),
        pltpu.make_async_copy(land_hbm, land_all.at[mine_l], own_sem.at[1]),
        pltpu.make_async_copy(lab_hbm, lab_all.at[mine_l], own_sem.at[2]),
    ]
    for c in local:
        c.start()

    peers = [(e, d) for e in range(n_hi) for d in range(n_z) if e or d]
    barrier = pltpu.get_barrier_semaphore()
    greet = [device(plus(hi, e, n_hi), lo, plus(z, d, n_z), core) for e, d in peers]
    greet += [device(hi, plus(lo, f, n_lo), z, core) for f in range(1, n_lo)]
    greet += [device(hi, lo, z, plus(core, s, n_core)) for s in range(1, n_core)]
    for dev in greet:
        pl.semaphore_signal(barrier, inc=1, device_id=dev, device_id_type=MESH)
    pl.semaphore_wait(barrier, len(greet))

    piece = land_rows // CHUNKS
    started = []

    def go(copy):
        copy.start()
        started.append(copy)

    def lx(src, slot, f, c):
        part_rows = pl.ds(c * piece, piece)
        return remote(
            src.at[part_rows],
            land_all.at[slot, part_rows],
            lx_send.at[f, c],
            lx_recv.at[f, c],
            device(hi, plus(lo, f, n_lo), z, core),
        )

    def bx(src, slot, f):
        return remote(
            src, lab_all.at[slot], bx_send.at[f], bx_recv.at[f], device(hi, plus(lo, f, n_lo), z, core)
        )

    def ls(src, slot, s, f, c):
        part_rows = pl.ds(c * piece, piece)
        return remote(
            src.at[part_rows],
            land_all.at[slot, part_rows],
            ls_send.at[s, f, c],
            ls_recv.at[s, f, c],
            device(hi, lo, z, plus(core, s, n_core)),
        )

    def bs(src, slot, s, f):
        return remote(
            src, lab_all.at[slot], bs_send.at[s, f], bs_recv.at[s, f], device(hi, lo, z, plus(core, s, n_core))
        )

    def qz(slot, d):
        return remote(
            q_hbm, q_all.at[slot], qz_send.at[d], qz_recv.at[d], device(hi, lo, plus(z, d, n_z), core)
        )

    def qy(src, slot, e, d):
        return remote(
            src, q_all.at[slot], qy_send.at[e, d], qy_recv.at[e, d], device(plus(hi, e, n_hi), lo, z, core)
        )

    for d in range(1, n_z):
        go(qz(mine_q, d))
    for f in range(1, n_lo):
        for c in range(CHUNKS):
            go(lx(land_hbm, mine_l, f, c))
        go(bx(lab_hbm, mine_l, f))
    for e in range(1, n_hi):
        go(qy(q_hbm, mine_q, e, 0))
    for s in range(1, n_core):
        for c in range(CHUNKS):
            go(ls(land_hbm, mine_l, s, 0, c))
        go(bs(lab_hbm, mine_l, s, 0))

    for d in range(1, n_z):
        slot = hi * n_z + plus(z, -d, n_z)
        qz(slot, d).wait_recv()
        for e in range(1, n_hi):
            go(qy(q_all.at[slot], slot, e, d))
    for f in range(1, n_lo):
        slot = plus(lo, -f, n_lo) * n_core + core
        for c in range(CHUNKS):
            lx(land_hbm, slot, f, c).wait_recv()
            for s in range(1, n_core):
                go(ls(land_all.at[slot], slot, s, f, c))
        bx(lab_hbm, slot, f).wait_recv()
        for s in range(1, n_core):
            go(bs(lab_all.at[slot], slot, s, f))
    for c in local:
        c.wait()
    for e in range(1, n_hi):
        for d in range(n_z):
            slot = plus(hi, -e, n_hi) * n_z + plus(z, -d, n_z)
            qy(q_hbm, slot, e, d).wait_recv()
    for f in range(n_lo):
        for s in range(1, n_core):
            slot = plus(lo, -f, n_lo) * n_core + plus(core, -s, n_core)
            for c in range(CHUNKS):
                ls(land_hbm, slot, s, f, c).wait_recv()
            bs(lab_hbm, slot, s, f).wait_recv()

    land = land_all[...].reshape(tiles * land_rows, width)
    labs = lab_all[...].reshape(tiles * land_rows, classes)
    land_f = land.astype(jnp.float32)
    square = land_f * land_f
    lanes = 128 if width % 128 == 0 else width
    folded = square[:, :lanes]
    for start in range(lanes, width, lanes):
        folded = folded + square[:, start : start + lanes]
    half_norm = 0.5 * jnp.sum(folded.T, axis=0, keepdims=True)
    scale_factor = 4.0 / math.sqrt(width)
    tile_of = lax.broadcasted_iota(jnp.int32, (1, tiles * land_rows), 1) // land_rows
    slab = n_z * rows
    lane = lax.broadcasted_iota(jnp.int32, (slab, classes), 1)

    def score(h, carry):
        flags = jnp.zeros((1, tiles * land_rows), jnp.int32)
        for t in range(tiles):
            source = (hi * n_lo + t // n_core) * n_grp + z * n_core + t % n_core
            flags = jnp.where(tile_of == t, mask_ref[h * n_lo + lo, source], flags)
        listed = flags > 0
        block = q_all[pl.ds(h * n_z, n_z)].reshape(slab, width)
        logits = lax.dot_general(
            block, land, (((1,), (1,)), ((), ())), preferred_element_type=jnp.float32
        )
        logits = (logits - half_norm) * scale_factor
        row_max = jnp.max(jnp.where(listed, logits, -1e30), axis=1, keepdims=True)
        weights = jnp.where(listed, jnp.exp(logits - row_max), 0.0)
        weight_sum = jnp.sum(weights, axis=1, keepdims=True)
        label_sum = jnp.dot(weights.astype(jnp.bfloat16), labs, preferred_element_type=jnp.float32)
        stats = jnp.zeros((slab, classes), jnp.float32)
        for i, term in enumerate(three_terms(row_max) + three_terms(weight_sum)):
            stats = jnp.where(lane == i, term, stats)
        message = jnp.concatenate([label_sum, stats], axis=1).astype(jnp.bfloat16)
        part[pl.ds(h * n_z, n_z)] = message.reshape(n_z, rows, 2 * classes)
        return carry

    lax.fori_loop(0, n_hi, score, 0, unroll=n_hi <= 4)

    def send_part(e, d, src, dst):
        return remote(
            part.at[src],
            got.at[dst],
            p_send.at[e, d],
            p_recv.at[e, d],
            device(plus(hi, e, n_hi), lo, plus(z, d, n_z), core),
        )

    for e, d in peers:
        go(send_part(e, d, plus(hi, e, n_hi) * n_z + plus(z, d, n_z), mine_q))
    got[mine_q] = part[mine_q]
    for e, d in peers:
        send_part(e, d, mine_q, plus(hi, -e, n_hi) * n_z + plus(z, -d, n_z)).wait_recv()

    parts = got[...].astype(jnp.float32)
    sums, stats = parts[:, :, :classes], parts[:, :, classes:]
    maxes = stats[:, :, 0:1] + stats[:, :, 1:2] + stats[:, :, 2:3]
    totals = stats[:, :, 3:4] + stats[:, :, 4:5] + stats[:, :, 5:6]
    keep = jnp.exp(maxes - jnp.max(maxes, axis=0, keepdims=True))
    out_ref[...] = jnp.sum(sums * keep, axis=0) / jnp.sum(totals * keep, axis=0)

    for copy in started:
        copy.wait_send()


def local(n_loop, n_grp, queries, landmarks, labels, tile_mask):
    n_lo = 2 if n_loop % 2 == 0 else 1
    n_core = 2 if n_grp % 2 == 0 else 1
    n_hi, n_z = n_loop // n_lo, n_grp // n_core
    rows, width = queries.shape
    land_rows, classes = labels.shape
    tiles = n_lo * n_core
    blocks = n_hi * n_z
    dma = pltpu.SemaphoreType.DMA
    any_space = pl.BlockSpec(memory_space=pl.ANY)
    scores = pl.pallas_call(
        functools.partial(kernel, (n_hi, n_lo, n_z, n_core)),
        out_shape=jax.ShapeDtypeStruct((rows, classes), jnp.float32),
        in_specs=[pl.BlockSpec(memory_space=pltpu.SMEM), any_space, any_space, any_space],
        out_specs=pl.BlockSpec(memory_space=pltpu.VMEM),
        scratch_shapes=[
            pltpu.VMEM((blocks, rows, width), jnp.bfloat16),
            pltpu.VMEM((tiles, land_rows, width), jnp.bfloat16),
            pltpu.VMEM((tiles, land_rows, classes), jnp.bfloat16),
            pltpu.VMEM((blocks, rows, 2 * classes), jnp.bfloat16),
            pltpu.VMEM((blocks, rows, 2 * classes), jnp.bfloat16),
            dma((3,)),
            dma((n_z,)),
            dma((n_z,)),
            dma((n_hi, n_z)),
            dma((n_hi, n_z)),
            dma((n_lo, CHUNKS)),
            dma((n_lo, CHUNKS)),
            dma((n_lo,)),
            dma((n_lo,)),
            dma((n_core, n_lo, CHUNKS)),
            dma((n_core, n_lo, CHUNKS)),
            dma((n_core, n_lo)),
            dma((n_core, n_lo)),
            dma((n_hi, n_z)),
            dma((n_hi, n_z)),
        ],
        compiler_params=pltpu.CompilerParams(
            collective_id=0, has_side_effects=True, vmem_limit_bytes=48 * 1024 * 1024
        ),
    )(tile_mask, queries, landmarks, labels)
    return scores.astype(jnp.bfloat16)


def solution(mesh):
    in_specs = (P(("loop", "grp"), None), P(("loop", "grp"), None), P(("loop", "grp"), None), P())
    out_specs = P(("loop", "grp"), None)
    body = functools.partial(local, mesh.shape["loop"], mesh.shape["grp"])
    return jax.shard_map(body, mesh=mesh, in_specs=in_specs, out_specs=out_specs, check_vma=False)
```

time: 70.3 us -> 25.1 us (0.36)
  blocking collectives: 50.2 us -> 0 us
  Pallas kernels: 0 us -> 21.1 us
  waiting for transfers between devices: 6.15 us -> 0 us
  starting transfers between devices: 4.66 us -> 0 us
  between operations: 2.6 us -> 0.01 us
  other arithmetic: 2.35 us -> 0.6 us
  matrix products: 1.68 us -> 0 us
  local copies, waits for them, and re-layouts: 2.22 us -> 3.06 us
    all_gather x4 -> x0, blocking collectives: 50.2 us -> none  [the longest x3 35.4 us: combined_all(): gathered = jax.tree.map(lambda a: lax.all_gather(a, axis), part)]
    pallas_call x0 -> x1, Pallas kernels: none -> 21.1 us  [local(): pl.pallas_call(functools.partial(kernel, (n_hi, n_lo, n_z, n_core)), out_...]
    ppermute x3 -> x0, waiting for transfers between devices: 6.15 us -> none  [from_behind(): return lax.ppermute(value, axis, pairs)]
    ppermute x3 -> x0, starting transfers between devices: 4.66 us -> none  [from_behind(): return lax.ppermute(value, axis, pairs)]
    dot_general x8 -> x0, matrix products: 1.68 us -> none  [the longest x4 0.89 us: absorb(): lax.dot_general(query_slab, land_rows, (((1,), (1,)), ((), ())), preferre...]
    unnamed x9 -> x8, local copies, waits for them, and re-layouts: 1.46 us -> 3.06 us
    add x14 -> x0, other arithmetic: 0.97 us -> none  [the longest x7 0.78 us: combine(): first_labels * first_keep[:, None] + second_labels * second_keep[:, None]]
    dynamic_slice x3 -> x0, local copies, waits for them, and re-layouts: 0.75 us -> none  [the longest x1 0.66 us: absorb(): lax.dynamic_index_in_dim(listed_row, source * n_grp + column, 0, keepdims...]
  transfers between devices with their start and end apart: 3 -> 0, of which waited for: 1 -> 0; matrix products, arithmetic and copies ran while one was open for 2% -> 0% of each run, Pallas kernels for 0% -> 0%
where the time goes in v1:
time: 25.1 us; the launch traced here: 24.8 us
  Pallas kernels  21.1 us (84%)
  local copies, waits for them, and re-layouts  3.06 us (12%)
  other arithmetic  0.6 us (2%)
    pallas_call x1, Pallas kernels, local(): pl.pallas_call(functools.partial(kernel, (n_hi, n_lo, n_z, n_core)), out_...  21.1 us
    unnamed x8, local copies, waits for them, and re-layouts  3.06 us
    convert_element_type x1, other arithmetic, local(): return scores.astype(jnp.bfloat16)  0.6 us

profile of v1, /device:TPU:0, one launch (start us, length us, event | category | flops | bytes accessed | tf_op | source)
XLA Modules:
  0.0 24.8 jit_solution(10732850267048104532)
XLA Ops:
  0.0 0.0 copy-start
  0.0 0.9 %copy-done = bf16[64,1024]{1,0:T(8,128)(2,1)S(1)} copy-done((bf16[64,1024]{1,0:T(8,128)(2,1)S(1)}, bf16[64,1024]{1,0:T(8,128)(2,1)}, u32[]{:S(2)}) %copy-start) | copy-done | bytes 131096
  0.9 0.0 copy-start.1
  0.9 0.8 %copy-done.1 = bf16[16,1024]{1,0:T(8,128)(2,1)S(1)} copy-done((bf16[16,1024]{1,0:T(8,128)(2,1)S(1)}, bf16[16,1024]{1,0:T(8,128)(2,1)}, u32[]{:S(2)}) %copy-start.1) | copy-done | bytes 32792
  1.7 0.0 copy-start.2
  1.7 0.7 %copy-done.2 = bf16[64,128]{1,0:T(8,128)(2,1)S(1)} copy-done((bf16[64,128]{1,0:T(8,128)(2,1)S(1)}, bf16[64,128]{1,0:T(8,128)(2,1)}, u32[]{:S(2)}) %copy-start.2) | copy-done | bytes 16408
  2.4 0.0 copy-start.3
  2.4 0.7 %copy-done.3 = s32[4,32]{1,0:T(4,128)S(1)} copy-done((s32[4,32]{1,0:T(4,128)S(1)}, s32[4,32]{1,0:T(4,128)}, u32[]{:S(2)}) %copy-start.3) | copy-done | bytes 536
  3.1 21.1 %shard_map.46 = f32[16,128]{1,0:T(8,128)S(1)} custom-call(s32[4,32]{1,0:T(4,128)S(1)} %copy-done.3, bf16[16,1024]{1,0:T(8,128)(2,1)S(1)} %copy-done.1, bf16[64,1024]{1,0:T(8,128)(2,1)S(1)} %copy-done, bf16[64,128]{1,0:T(8,128)(2,1)S(1)} %copy-done.2), custom_call_target="tpu_custom_call" | custom-call | tf_op jit(solution)/shard_map/pallas_call | solution.py:253
  24.2 0.6 %convert_element_type.3 = bf16[16,128]{1,0:T(8,128)(2,1)} convert(f32[16,128]{1,0:T(8,128)S(1)} %shard_map.46) | non-fusion elementwise | flops 2048 | bytes 12288 | tf_op jit(solution)/shard_map/convert_element_type | solution.py:284
Async XLA Ops:
  0.0 0.9 %copy-start = (bf16[64,1024]{1,0:T(8,128)(2,1)S(1)}, bf16[64,1024]{1,0:T(8,128)(2,1)}, u32[]{:S(2)}) copy-start(bf16[64,1024]{1,0:T(8,128)(2,1)} %land_hbm.1) | copy-start | bytes 393220
  0.9 0.8 %copy-start.1 = (bf16[16,1024]{1,0:T(8,128)(2,1)S(1)}, bf16[16,1024]{1,0:T(8,128)(2,1)}, u32[]{:S(2)}) copy-start(bf16[16,1024]{1,0:T(8,128)(2,1)} %q_hbm.1) | copy-start | bytes 98308
  1.7 0.7 %copy-start.2 = (bf16[64,128]{1,0:T(8,128)(2,1)S(1)}, bf16[64,128]{1,0:T(8,128)(2,1)}, u32[]{:S(2)}) copy-start(bf16[64,128]{1,0:T(8,128)(2,1)} %lab_hbm.1) | copy-start | bytes 49156
  2.4 0.7 %copy-start.3 = (s32[4,32]{1,0:T(4,128)S(1)}, s32[4,32]{1,0:T(4,128)}, u32[]{:S(2)}) copy-start(s32[4,32]{1,0:T(4,128)} %mask_ref.1) | copy-start | bytes 1540

commit v2 on v1

--- a/solution.py
+++ b/solution.py
@@ -22,11 +22,13 @@
 
 def kernel(
     dims,
-    mask_ref,
+    mask_hbm,
     q_hbm,
     land_hbm,
     lab_hbm,
     out_ref,
+    mask_ref,
+    fold,
     q_all,
     land_all,
     lab_all,
@@ -72,14 +74,6 @@
 
     mine_q = hi * n_z + z
     mine_l = lo * n_core + core
-    local = [
-        pltpu.make_async_copy(q_hbm, q_all.at[mine_q], own_sem.at[0]),
-        pltpu.make_async_copy(land_hbm, land_all.at[mine_l], own_sem.at[1]),
-        pltpu.make_async_copy(lab_hbm, lab_all.at[mine_l], own_sem.at[2]),
-    ]
-    for c in local:
-        c.start()
-
     peers = [(e, d) for e in range(n_hi) for d in range(n_z) if e or d]
     barrier = pltpu.get_barrier_semaphore()
     greet = [device(plus(hi, e, n_hi), lo, plus(z, d, n_z), core) for e, d in peers]
@@ -87,6 +81,14 @@
     greet += [device(hi, lo, z, plus(core, s, n_core)) for s in range(1, n_core)]
     for dev in greet:
         pl.semaphore_signal(barrier, inc=1, device_id=dev, device_id_type=MESH)
+    local = [
+        pltpu.make_async_copy(q_hbm, q_all.at[mine_q], own_sem.at[0]),
+        pltpu.make_async_copy(land_hbm, land_all.at[mine_l], own_sem.at[1]),
+        pltpu.make_async_copy(lab_hbm, lab_all.at[mine_l], own_sem.at[2]),
+        pltpu.make_async_copy(mask_hbm, mask_ref, own_sem.at[3]),
+    ]
+    for c in local:
+        c.start()
     pl.semaphore_wait(barrier, len(greet))
 
     piece = land_rows // CHUNKS
@@ -95,6 +97,15 @@
     def go(copy):
         copy.start()
         started.append(copy)
+
+    def square_sums(slot):
+        land_f = land_all[slot].astype(jnp.float32)
+        square = land_f * land_f
+        lanes = fold.shape[2]
+        total = square[:, :lanes]
+        for start in range(lanes, width, lanes):
+            total = total + square[:, start : start + lanes]
+        fold[slot] = total
 
     def lx(src, slot, f, c):
         part_rows = pl.ds(c * piece, piece)
@@ -148,6 +159,10 @@
         for c in range(CHUNKS):
             go(ls(land_hbm, mine_l, s, 0, c))
         go(bs(lab_hbm, mine_l, s, 0))
+
+    for c in local:
+        c.wait()
+    square_sums(mine_l)
 
     for d in range(1, n_z):
         slot = hi * n_z + plus(z, -d, n_z)
@@ -163,40 +178,42 @@
         bx(lab_hbm, slot, f).wait_recv()
         for s in range(1, n_core):
             go(bs(lab_all.at[slot], slot, s, f))
-    for c in local:
-        c.wait()
-    for e in range(1, n_hi):
-        for d in range(n_z):
-            slot = plus(hi, -e, n_hi) * n_z + plus(z, -d, n_z)
-            qy(q_hbm, slot, e, d).wait_recv()
+    for f in range(1, n_lo):
+        square_sums(plus(lo, -f, n_lo) * n_core + core)
     for f in range(n_lo):
         for s in range(1, n_core):
             slot = plus(lo, -f, n_lo) * n_core + plus(core, -s, n_core)
             for c in range(CHUNKS):
                 ls(land_hbm, slot, s, f, c).wait_recv()
             bs(lab_hbm, slot, s, f).wait_recv()
+            square_sums(slot)
+    for e in range(1, n_hi):
+        for d in range(n_z):
+            slot = plus(hi, -e, n_hi) * n_z + plus(z, -d, n_z)
+            qy(q_hbm, slot, e, d).wait_recv()
 
     land = land_all[...].reshape(tiles * land_rows, width)
     labs = lab_all[...].reshape(tiles * land_rows, classes)
-    land_f = land.astype(jnp.float32)
-    square = land_f * land_f
-    lanes = 128 if width % 128 == 0 else width
-    folded = square[:, :lanes]
-    for start in range(lanes, width, lanes):
-        folded = folded + square[:, start : start + lanes]
-    half_norm = 0.5 * jnp.sum(folded.T, axis=0, keepdims=True)
+    half_norm = 0.5 * jnp.sum(fold[...].reshape(tiles * land_rows, -1).T, axis=0, keepdims=True)
     scale_factor = 4.0 / math.sqrt(width)
     tile_of = lax.broadcasted_iota(jnp.int32, (1, tiles * land_rows), 1) // land_rows
     slab = n_z * rows
-    lane = lax.broadcasted_iota(jnp.int32, (slab, classes), 1)
-
-    def score(h, carry):
-        flags = jnp.zeros((1, tiles * land_rows), jnp.int32)
-        for t in range(tiles):
-            source = (hi * n_lo + t // n_core) * n_grp + z * n_core + t % n_core
-            flags = jnp.where(tile_of == t, mask_ref[h * n_lo + lo, source], flags)
+    group = n_hi if n_hi <= 2 else 1
+    lane = lax.broadcasted_iota(jnp.int32, (group * slab, classes), 1)
+    row = lax.broadcasted_iota(jnp.int32, (group * slab, tiles * land_rows), 0)
+
+    def score(step, carry):
+        flags = jnp.zeros((group * slab, tiles * land_rows), jnp.int32)
+        for i in range(group):
+            of_row = jnp.zeros((1, tiles * land_rows), jnp.int32)
+            for t in range(tiles):
+                source = (hi * n_lo + t // n_core) * n_grp + z * n_core + t % n_core
+                value = mask_ref[(step * group + i) * n_lo + lo, source]
+                of_row = jnp.where(tile_of == t, value, of_row)
+            flags = jnp.where(row >= i * slab, of_row, flags)
         listed = flags > 0
-        block = q_all[pl.ds(h * n_z, n_z)].reshape(slab, width)
+        here = pl.ds(step * (group * n_z), group * n_z)
+        block = q_all[here].reshape(group * slab, width)
         logits = lax.dot_general(
             block, land, (((1,), (1,)), ((), ())), preferred_element_type=jnp.float32
         )
@@ -205,14 +222,14 @@
         weights = jnp.where(listed, jnp.exp(logits - row_max), 0.0)
         weight_sum = jnp.sum(weights, axis=1, keepdims=True)
         label_sum = jnp.dot(weights.astype(jnp.bfloat16), labs, preferred_element_type=jnp.float32)
-        stats = jnp.zeros((slab, classes), jnp.float32)
+        stats = jnp.zeros((group * slab, classes), jnp.float32)
         for i, term in enumerate(three_terms(row_max) + three_terms(weight_sum)):
             stats = jnp.where(lane == i, term, stats)
         message = jnp.concatenate([label_sum, stats], axis=1).astype(jnp.bfloat16)
-        part[pl.ds(h * n_z, n_z)] = message.reshape(n_z, rows, 2 * classes)
+        part[here] = message.reshape(group * n_z, rows, 2 * classes)
         return carry
 
-    lax.fori_loop(0, n_hi, score, 0, unroll=n_hi <= 4)
+    lax.fori_loop(0, n_hi // group, score, 0)
 
     def send_part(e, d, src, dst):
         return remote(
@@ -248,20 +265,23 @@
     land_rows, classes = labels.shape
     tiles = n_lo * n_core
     blocks = n_hi * n_z
+    lanes = 128 if width % 128 == 0 else width
     dma = pltpu.SemaphoreType.DMA
-    any_space = pl.BlockSpec(memory_space=pl.ANY)
+    any_space = pl.BlockSpec(memory_space=pltpu.HBM)
     scores = pl.pallas_call(
         functools.partial(kernel, (n_hi, n_lo, n_z, n_core)),
         out_shape=jax.ShapeDtypeStruct((rows, classes), jnp.float32),
-        in_specs=[pl.BlockSpec(memory_space=pltpu.SMEM), any_space, any_space, any_space],
+        in_specs=[any_space] * 4,
         out_specs=pl.BlockSpec(memory_space=pltpu.VMEM),
         scratch_shapes=[
+            pltpu.SMEM(tile_mask.shape, jnp.int32),
+            pltpu.VMEM((tiles, land_rows, lanes), jnp.float32),
             pltpu.VMEM((blocks, rows, width), jnp.bfloat16),
             pltpu.VMEM((tiles, land_rows, width), jnp.bfloat16),
             pltpu.VMEM((tiles, land_rows, classes), jnp.bfloat16),
             pltpu.VMEM((blocks, rows, 2 * classes), jnp.bfloat16),
             pltpu.VMEM((blocks, rows, 2 * classes), jnp.bfloat16),
-            dma((3,)),
+            dma((4,)),
             dma((n_z,)),
             dma((n_z,)),
             dma((n_hi, n_z)),
@@ -278,7 +298,7 @@
             dma((n_hi, n_z)),
         ],
         compiler_params=pltpu.CompilerParams(
-            collective_id=0, has_side_effects=True, vmem_limit_bytes=48 * 1024 * 1024
+            collective_id=0, has_side_effects=True, vmem_limit_bytes=60 * 1024 * 1024
         ),
     )(tile_mask, queries, landmarks, labels)
     return scores.astype(jnp.bfloat16)

time: 25.1 us -> 22 us (0.88)
  local copies, waits for them, and re-layouts: 3.06 us -> 0 us
  other arithmetic: 0.6 us -> 1.29 us
  Pallas kernels: 21.1 us -> 20.5 us
    unnamed x8 -> x0, local copies, waits for them, and re-layouts: 3.06 us -> none
    convert_element_type x1, other arithmetic: 0.6 us -> 1.29 us  [local(): return scores.astype(jnp.bfloat16)]
    pallas_call x1, Pallas kernels: 21.1 us -> 20.5 us  [local(): pl.pallas_call(functools.partial(kernel, (n_hi, n_lo, n_z, n_core)), out_...]
where the time goes in v2:
time: 22 us; the launch traced here: 21.8 us
  Pallas kernels  20.5 us (93%)
  other arithmetic  1.29 us (6%)
    pallas_call x1, Pallas kernels, local(): pl.pallas_call(functools.partial(kernel, (n_hi, n_lo, n_z, n_core)), out_...  20.5 us
    convert_element_type x1, other arithmetic, local(): return scores.astype(jnp.bfloat16)  1.29 us

profile of v2, /device:TPU:0, one launch (start us, length us, event | category | flops | bytes accessed | tf_op | source)
XLA Modules:
  0.0 21.8 jit_solution(1586272477235710966)
XLA Ops:
  0.0 20.5 %shard_map.46 = f32[16,128]{1,0:T(8,128)} custom-call(s32[4,32]{1,0:T(4,128)} %mask_hbm.1, bf16[16,1024]{1,0:T(8,128)(2,1)} %q_hbm.1, bf16[64,1024]{1,0:T(8,128)(2,1)} %land_hbm.1, bf16[64,128]{1,0:T(8,128)(2,1)} %lab_hbm.1), custom_call_target="tpu_custom_call" | custom-call | tf_op jit(solution)/shard_map/pallas_call | solution.py:271
  20.5 1.3 %convert_element_type.3 = bf16[16,128]{1,0:T(8,128)(2,1)} convert(f32[16,128]{1,0:T(8,128)} %shard_map.46) | non-fusion elementwise | flops 2048 | bytes 12288 | tf_op jit(solution)/shard_map/convert_element_type | solution.py:304

commit v3 on v2

--- a/solution.py
+++ b/solution.py
@@ -9,7 +9,7 @@
 from jax.sharding import PartitionSpec as P
 
 MESH = pl.DeviceIdType.MESH
-CHUNKS = 2
+CHUNKS = 1
 
 
 def three_terms(value):
@@ -67,6 +67,20 @@
     def plus(a, d, n):
         return lax.rem(a + d + n, n)
 
+    def partner(a, d, n, sign):
+        if n & (n - 1):
+            return plus(a, sign * d, n)
+        for bit in range(n.bit_length()):
+            if d >> bit & 1:
+                a = a + (1 << bit) * (1 - 2 * lax.rem(a // (1 << bit), 2))
+        return a
+
+    def z_to(d):
+        return partner(z, d, n_z, 1)
+
+    def z_from(d):
+        return partner(z, d, n_z, -1)
+
     def remote(src, dst, send, recv, dev):
         return pltpu.make_async_remote_copy(
             src_ref=src, dst_ref=dst, send_sem=send, recv_sem=recv, device_id=dev, device_id_type=MESH
@@ -74,9 +88,10 @@
 
     mine_q = hi * n_z + z
     mine_l = lo * n_core + core
-    peers = [(e, d) for e in range(n_hi) for d in range(n_z) if e or d]
+    peers = [(e, d) for d in reversed(range(n_z)) for e in reversed(range(n_hi)) if e or d]
     barrier = pltpu.get_barrier_semaphore()
-    greet = [device(plus(hi, e, n_hi), lo, plus(z, d, n_z), core) for e, d in peers]
+    greet = [device(hi, lo, z_to(d), core) for d in reversed(range(1, n_z))]
+    greet += [device(plus(hi, e, n_hi), lo, z, core) for e in range(1, n_hi)]
     greet += [device(hi, plus(lo, f, n_lo), z, core) for f in range(1, n_lo)]
     greet += [device(hi, lo, z, plus(core, s, n_core)) for s in range(1, n_core)]
     for dev in greet:
@@ -139,7 +154,7 @@
 
     def qz(slot, d):
         return remote(
-            q_hbm, q_all.at[slot], qz_send.at[d], qz_recv.at[d], device(hi, lo, plus(z, d, n_z), core)
+            q_hbm, q_all.at[slot], qz_send.at[d], qz_recv.at[d], device(hi, lo, z_to(d), core)
         )
 
     def qy(src, slot, e, d):
@@ -147,7 +162,7 @@
             src, q_all.at[slot], qy_send.at[e, d], qy_recv.at[e, d], device(plus(hi, e, n_hi), lo, z, core)
         )
 
-    for d in range(1, n_z):
+    for d in reversed(range(1, n_z)):
         go(qz(mine_q, d))
     for f in range(1, n_lo):
         for c in range(CHUNKS):
@@ -165,7 +180,7 @@
     square_sums(mine_l)
 
     for d in range(1, n_z):
-        slot = hi * n_z + plus(z, -d, n_z)
+        slot = hi * n_z + z_from(d)
         qz(slot, d).wait_recv()
         for e in range(1, n_hi):
             go(qy(q_all.at[slot], slot, e, d))
@@ -189,7 +204,7 @@
             square_sums(slot)
     for e in range(1, n_hi):
         for d in range(n_z):
-            slot = plus(hi, -e, n_hi) * n_z + plus(z, -d, n_z)
+            slot = plus(hi, -e, n_hi) * n_z + z_from(d)
             qy(q_hbm, slot, e, d).wait_recv()
 
     land = land_all[...].reshape(tiles * land_rows, width)
@@ -237,14 +252,14 @@
             got.at[dst],
             p_send.at[e, d],
             p_recv.at[e, d],
-            device(plus(hi, e, n_hi), lo, plus(z, d, n_z), core),
+            device(plus(hi, e, n_hi), lo, z_to(d), core),
         )
 
     for e, d in peers:
-        go(send_part(e, d, plus(hi, e, n_hi) * n_z + plus(z, d, n_z), mine_q))
+        go(send_part(e, d, plus(hi, e, n_hi) * n_z + z_to(d), mine_q))
     got[mine_q] = part[mine_q]
     for e, d in peers:
-        send_part(e, d, mine_q, plus(hi, -e, n_hi) * n_z + plus(z, -d, n_z)).wait_recv()
+        send_part(e, d, mine_q, plus(hi, -e, n_hi) * n_z + z_from(d)).wait_recv()
 
     parts = got[...].astype(jnp.float32)
     sums, stats = parts[:, :, :classes], parts[:, :, classes:]

time: 22 us -> 20.6 us (0.936)
  Pallas kernels: 20.5 us -> 19.1 us
    pallas_call x1, Pallas kernels: 20.5 us -> 19.1 us  [local(): pl.pallas_call(functools.partial(kernel, (n_hi, n_lo, n_z, n_core)), out_...]
where the time goes in v3:
time: 20.6 us; the launch traced here: 20.4 us
  Pallas kernels  19.1 us (93%)
  other arithmetic  1.29 us (6%)
    pallas_call x1, Pallas kernels, local(): pl.pallas_call(functools.partial(kernel, (n_hi, n_lo, n_z, n_core)), out_...  19.1 us
    convert_element_type x1, other arithmetic, local(): return scores.astype(jnp.bfloat16)  1.29 us

profile of v3, /device:TPU:0, one launch (start us, length us, event | category | flops | bytes accessed | tf_op | source)
XLA Modules:
  0.0 20.4 jit_solution(16505725345999332238)
XLA Ops:
  0.0 19.1 %shard_map.46 = f32[16,128]{1,0:T(8,128)} custom-call(s32[4,32]{1,0:T(4,128)} %mask_hbm.1, bf16[16,1024]{1,0:T(8,128)(2,1)} %q_hbm.1, bf16[64,1024]{1,0:T(8,128)(2,1)} %land_hbm.1, bf16[64,128]{1,0:T(8,128)(2,1)} %lab_hbm.1), custom_call_target="tpu_custom_call" | custom-call | tf_op jit(solution)/shard_map/pallas_call | solution.py:286
  19.1 1.3 %convert_element_type.3 = bf16[16,128]{1,0:T(8,128)(2,1)} convert(f32[16,128]{1,0:T(8,128)} %shard_map.46) | non-fusion elementwise | flops 2048 | bytes 12288 | tf_op jit(solution)/shard_map/convert_element_type | solution.py:319

commit v4 on v3

--- a/solution.py
+++ b/solution.py
@@ -162,7 +162,7 @@
             src, q_all.at[slot], qy_send.at[e, d], qy_recv.at[e, d], device(plus(hi, e, n_hi), lo, z, core)
         )
 
-    for d in reversed(range(1, n_z)):
+    for d in range(1, n_z):
         go(qz(mine_q, d))
     for f in range(1, n_lo):
         for c in range(CHUNKS):

time: 20.6 us -> 20.4 us (level)
    pallas_call x1, Pallas kernels: 19.1 us -> 18.9 us  [local(): pl.pallas_call(functools.partial(kernel, (n_hi, n_lo, n_z, n_core)), out_...]
where the time goes in v4:
time: 20.4 us; the launch traced here: 20.2 us
  Pallas kernels  18.9 us (93%)
  other arithmetic  1.29 us (6%)
    pallas_call x1, Pallas kernels, local(): pl.pallas_call(functools.partial(kernel, (n_hi, n_lo, n_z, n_core)), out_...  18.9 us
    convert_element_type x1, other arithmetic, local(): return scores.astype(jnp.bfloat16)  1.29 us

profile of v4, /device:TPU:0, one launch (start us, length us, event | category | flops | bytes accessed | tf_op | source)
XLA Modules:
  0.0 20.2 jit_solution(14477227354207481625)
XLA Ops:
  0.0 18.9 %shard_map.46 = f32[16,128]{1,0:T(8,128)} custom-call(s32[4,32]{1,0:T(4,128)} %mask_hbm.1, bf16[16,1024]{1,0:T(8,128)(2,1)} %q_hbm.1, bf16[64,1024]{1,0:T(8,128)(2,1)} %land_hbm.1, bf16[64,128]{1,0:T(8,128)(2,1)} %lab_hbm.1), custom_call_target="tpu_custom_call" | custom-call | tf_op jit(solution)/shard_map/pallas_call | solution.py:286
  18.9 1.3 %convert_element_type.3 = bf16[16,128]{1,0:T(8,128)(2,1)} convert(f32[16,128]{1,0:T(8,128)} %shard_map.46) | non-fusion elementwise | flops 2048 | bytes 12288 | tf_op jit(solution)/shard_map/convert_element_type | solution.py:319
